TPU v7x, 256 devices: a whole 4x4x8 slice. The times are simulated.
256 devices in a mesh: mp: 8 (over z), hidden: 32 (over y, x, core).
Axes of the slice: x: 4, y: 4, z: 8, core: 2. Of those that a mesh axis runs over, the one named last changes fastest.
Arguments:
- inputs: bfloat16 [768, 18432], P('hidden', 'mp'), may hold values from -6 to 6
- gate_weight: bfloat16 [18432, 12288], P('mp', 'hidden'), may hold values from -0.046875 to 0.046875
- up_weight: bfloat16 [18432, 12288], P('mp', 'hidden'), may hold values from -0.046875 to 0.046875
- down_weight: bfloat16 [12288, 18432], P('hidden', 'mp'), may hold values from -0.0546875 to 0.0546875
- cotangent: bfloat16 [768, 18432], P('hidden', 'mp'), may hold values from -6 to 6
Outputs:
- grad_inputs: bfloat16 [768, 18432], P('hidden', 'mp')
- grad_gate: bfloat16 [18432, 12288], P('mp', 'hidden')
- grad_up: bfloat16 [18432, 12288], P('mp', 'hidden')
- grad_down: bfloat16 [12288, 18432], P('hidden', 'mp')
All inputs are finite; a program needn't handle non-finite values.
Results may differ from a plain program's by a relative error of at most 0.02.
Values may be sent and summed in bfloat16 or wider, within the bound.
A program may use at most 128 MiB of HBM per device.

v0:
```python
import jax
import jax.numpy as jnp
from jax import lax
from jax.sharding import PartitionSpec as P


def activate(gate, up, dhid):
    sig = jax.nn.sigmoid(gate)
    hidden_act = (gate * sig * up).astype(jnp.bfloat16)
    dup = (dhid * gate * sig).astype(jnp.bfloat16)
    dgate = (dhid * up * sig * (1.0 + gate * (1.0 - sig))).astype(jnp.bfloat16)
    return (hidden_act, dgate, dup)


def shards(inputs, gate_weight, up_weight, down_weight, cotangent):
    rows_in = lax.all_gather(inputs, "hidden", axis=0, tiled=True)
    gate_term = jnp.dot(rows_in, gate_weight, preferred_element_type=jnp.float32)
    up_term = jnp.dot(rows_in, up_weight, preferred_element_type=jnp.float32)
    rows_cot = lax.all_gather(cotangent, "hidden", axis=0, tiled=True)
    down_term = lax.dot_general(
        rows_cot, down_weight, (((1,), (1,)), ((), ())), preferred_element_type=jnp.float32
    )
    gate, up, dhid = lax.psum((gate_term, up_term, down_term), "mp")
    hidden_act, dgate, dup = activate(gate, up, dhid)
    contract_rows = (((0,), (0,)), ((), ()))
    grad_down = lax.dot_general(
        hidden_act, rows_cot, contract_rows, preferred_element_type=jnp.float32
    ).astype(jnp.bfloat16)
    grad_gate = lax.dot_general(
        rows_in, dgate, contract_rows, preferred_element_type=jnp.float32
    ).astype(jnp.bfloat16)
    grad_up = lax.dot_general(
        rows_in, dup, contract_rows, preferred_element_type=jnp.float32
    ).astype(jnp.bfloat16)
    first = lax.dot_general(
        dgate, gate_weight, (((1,), (1,)), ((), ())), preferred_element_type=jnp.float32
    )
    second = lax.dot_general(
        dup, up_weight, (((1,), (1,)), ((), ())), preferred_element_type=jnp.float32
    )
    grad_inputs = lax.psum_scatter(
        (first + second).astype(jnp.bfloat16), "hidden", scatter_dimension=0, tiled=True
    )
    return (grad_inputs, grad_gate, grad_up, grad_down)


def solution(mesh):
    placed = (
        P("hidden", "mp"),
        P("mp", "hidden"),
        P("mp", "hidden"),
        P("hidden", "mp"),
        P("hidden", "mp"),
    )
    return jax.shard_map(
        shards,
        mesh=mesh,
        in_specs=placed,
        out_specs=(P("hidden", "mp"), P("mp", "hidden"), P("mp", "hidden"), P("hidden", "mp")),
        check_vma=False,
    )
```

profile of v0, /device:TPU:1, one launch (start us, length us, event | category | flops | bytes accessed | tf_op | source)
XLA Modules:
  0.0 321.5 jit_solution(6820254041707909823)
XLA Ops:
  7.2 0.0 copy-start
  7.2 0.0 all-gather.5.cloned.1.call-start
  7.2 0.7 all-gather.5.cloned.1.call-update
  7.9 0.0 all-gather.3.cloned.1.call-start
  8.0 0.7 all-gather.3.cloned.1.call-update
  8.7 0.0 copy-start.1
  8.7 0.0 all-reduce.3.cloned.1.call-start
  8.7 56.8 %all-gather.5.cloned.1.call-done = bf16[768,2304]{1,0:T(8,128)(2,1)} async-done(((bf16[24,2304]{1,0:T(8,128)(2,1)}), bf16[768,2304]{1,0:T(8,128)(2,1)}) %all-gather.5.cloned.1.call-update) | async-done | bytes 3538960 | tf_op jit(solution)/shard_map/all_gather | solution.py:16
  65.6 0.0 copy-done
  65.6 0.0 copy-start.4
  65.6 5.2 %fusion.6 = f32[768,384]{1,0:T(8,128)} fusion(bf16[768,2304]{1,0:T(8,128)(2,1)} %all-gather.5.cloned.1.call-done, bf16[2304,384]{1,0:T(8,128)(2,1)S(1)} %copy-done), kind=kOutput, calls=%fused_computation.14 | convolution fusion | flops 1358954496 | bytes 6488064 | tf_op jit(solution)/shard_map/dot_general | solution.py:17
  70.7 0.0 copy-done.1
  70.7 0.0 copy-done.4
  70.7 3.0 fusion.5
  73.7 44.6 %all-gather.3.cloned.1.call-done = bf16[768,2304]{1,0:T(8,128)(2,1)} async-done(((bf16[24,2304]{1,0:T(8,128)(2,1)}), bf16[768,2304]{1,0:T(8,128)(2,1)}) %all-gather.3.cloned.1.call-update) | async-done | bytes 3538960 | tf_op jit(solution)/shard_map/all_gather | solution.py:19
  118.3 5.6 %fusion.4 = f32[768,384]{1,0:T(8,128)} fusion(bf16[768,2304]{1,0:T(8,128)(2,1)} %all-gather.3.cloned.1.call-done, bf16[384,2304]{1,0:T(8,128)(2,1)} %param.8), kind=kOutput, calls=%fused_computation.12 | convolution fusion | flops 1358954496 | bytes 6488064 | tf_op jit(solution)/shard_map/dot_general | solution.py:20
  123.9 0.0 all-reduce.3.cloned.1.call-update
  123.9 0.0 reduce-scatter.2.cloned.1.call-start
  124.0 97.1 %all-reduce.3.cloned.1.call-done = (f32[768,384]{1,0:T(8,128)}, f32[768,384]{1,0:T(8,128)}, f32[768,384]{1,0:T(8,128)}) async-done(((f32[768,384]{1,0:T(8,128)}, f32[768,384]{1,0:T(8,128)}, f32[768,384]{1,0:T(8,128)}), (f32[768,384]{1,0:T(8,128)}, f32[768,384]{1,0:T(8,128)}, f32[768,384]{1,0:T(8,128)})) %all-reduce.3.cloned.1.call-update) | async-done | bytes 3538960 | tf_op jit(solution)/shard_map/psum | solution.py:23
  221.0 2.5 multiply_convert_fusion.1
  223.6 0.0 copy-start.2
  223.6 2.0 fusion.7
  225.6 0.0 copy-done.2
  225.6 3.9 %add_convert_fusion = bf16[768,2304]{1,0:T(8,128)(2,1)} fusion(f32[768,2304]{1,0:T(8,128)S(1)} %fusion.7, bf16[768,384]{1,0:T(8,128)(2,1)S(1)} %get-tuple-element.11, bf16[2304,384]{1,0:T(8,128)(2,1)S(1)} %copy-done.2), kind=kOutput, calls=%fused_computation | convolution fusion | flops 1362493440 | bytes 12976128 | tf_op jit(solution)/shard_map/dot_general | solution.py:38
  229.6 0.0 reduce-scatter.2.cloned.1.call-update
  229.6 4.8 %fusion = bf16[2304,384]{0,1:T(8,128)(2,1)} fusion(bf16[768,384]{1,0:T(8,128)(2,1)S(1)} %get-tuple-element.12, bf16[768,2304]{1,0:T(8,128)(2,1)} %all-gather.5.cloned.1.call-done), kind=kOutput, calls=%fused_computation.4 | convolution fusion | flops 1359839232 | bytes 5898240 | tf_op jit(solution)/shard_map/dot_general | solution.py:29
  234.4 3.9 %copy.9 = bf16[2304,384]{1,0:T(8,128)(2,1)} copy(bf16[2304,384]{0,1:T(8,128)(2,1)} %fusion) | data formatting | bytes 3538944
  238.2 4.9 %fusion.1 = bf16[2304,384]{0,1:T(8,128)(2,1)} fusion(bf16[768,384]{1,0:T(8,128)(2,1)S(1)} %get-tuple-element.11, bf16[768,2304]{1,0:T(8,128)(2,1)} %all-gather.5.cloned.1.call-done), kind=kOutput, calls=%fused_computation.5 | convolution fusion | flops 1359839232 | bytes 5898240 | tf_op jit(solution)/shard_map/dot_general | solution.py:32
  243.1 0.0 copy-start.3
  243.1 4.0 %copy.10 = bf16[2304,384]{1,0:T(8,128)(2,1)} copy(bf16[2304,384]{0,1:T(8,128)(2,1)} %fusion.1) | data formatting | bytes 3538944
  247.1 0.0 copy-done.3
  247.1 5.3 %convolution_convert_fusion = bf16[384,2304]{1,0:T(8,128)(2,1)} fusion(bf16[768,2304]{1,0:T(8,128)(2,1)} %all-gather.3.cloned.1.call-done, f32[768,384]{1,0:T(8,128)} %get-tuple-element.10, f32[768,384]{1,0:T(8,128)S(1)} %copy-done.3), kind=kOutput, calls=%fused_computation.1 | convolution fusion | flops 1361608704 | bytes 7667712 | tf_op jit(solution)/shard_map/dot_general | solution.py:26
  252.4 62.6 %reduce-scatter.2.cloned.1.call-done = bf16[24,2304]{1,0:T(8,128)(2,1)} async-done(((bf16[768,2304]{1,0:T(8,128)(2,1)}), bf16[24,2304]{1,0:T(8,128)(2,1)}) %reduce-scatter.2.cloned.1.call-update) | async-done | bytes 110608 | tf_op jit(solution)/shard_map/reduce_scatter | solution.py:41
Async XLA Ops:
  7.2 58.4 %copy-start = (bf16[2304,384]{1,0:T(8,128)(2,1)S(1)}, bf16[2304,384]{1,0:T(8,128)(2,1)}, u32[]{:S(2)}) copy-start(bf16[2304,384]{1,0:T(8,128)(2,1)} %param.6) | copy-start | bytes 5308420
  7.2 58.4 %all-gather.5.cloned.1.call-start = ((), (), s32[]{:S(2)}) async-start(), calls=%async_computation.2 | async-start | bytes 3649536 | tf_op jit(solution)/shard_map/all_gather | solution.py:16
  7.9 110.4 %all-gather.3.cloned.1.call-start = ((), (), s32[]{:S(2)}) async-start(), calls=%async_computation.1 | async-start | bytes 3649536 | tf_op jit(solution)/shard_map/all_gather | solution.py:19
  8.7 62.1 %copy-start.1 = (bf16[2304,384]{1,0:T(8,128)(2,1)S(1)}, bf16[2304,384]{1,0:T(8,128)(2,1)}, u32[]{:S(2)}) copy-start(bf16[2304,384]{1,0:T(8,128)(2,1)} %param.7) | copy-start | bytes 5308420
  8.7 212.4 %all-reduce.3.cloned.1.call-start = ((), (), s32[]{:S(2)}) async-start(), calls=%async_computation.4 | async-start | bytes 7077888 | tf_op jit(solution)/shard_map/psum | solution.py:23
  65.6 5.2 %copy-start.4 = (bf16[768,2304]{1,0:T(8,128)(2,1)S(1)}, bf16[768,2304]{1,0:T(8,128)(2,1)}, u32[]{:S(2)}) copy-start(bf16[768,2304]{1,0:T(8,128)(2,1)} %all-gather.5.cloned.1.call-done) | copy-start | bytes 10616836
  123.9 191.0 %reduce-scatter.2.cloned.1.call-start = ((), (), s32[]{:S(2)}) async-start(), calls=%async_computation.3 | async-start | bytes 3649536 | tf_op jit(solution)/shard_map/reduce_scatter | solution.py:41
  223.6 2.0 copy-start.2
  243.1 4.0 %copy-start.3 = (f32[768,384]{1,0:T(8,128)S(1)}, f32[768,384]{1,0:T(8,128)}, u32[]{:S(2)}) copy-start(f32[768,384]{1,0:T(8,128)} %get-tuple-element.8) | copy-start | bytes 3538948
Sparse Core Ops, SparseCore 0:
  10.6 54.8 all-gather.4
  68.2 50.1 all-gather.2
  124.0 96.9 all-reduce.2
  229.7 85.1 reduce-scatter.1
where the time goes:
time: 322 us; the launch traced here: 321 us
  waiting for transfers between devices  262 us (81%)
  matrix products  34.7 us (11%)
  between operations  13.8 us (4%)
  local copies, waits for them, and re-layouts  7.85 us (2%)
    psum x1, waiting for transfers between devices, shards(): gate, up, dhid = lax.psum((gate_term, up_term, down_term), 'mp')  97.1 us
    reduce_scatter x1, waiting for transfers between devices, shards(): lax.psum_scatter((first + second).astype(jnp.bfloat16), 'hidden', scatter...  62.6 us
    all_gather x1, waiting for transfers between devices, shards(): rows_in = lax.all_gather(inputs, 'hidden', axis=0, tiled=True)  56.8 us
    all_gather x1, waiting for transfers between devices, shards(): rows_cot = lax.all_gather(cotangent, 'hidden', axis=0, tiled=True)  44.6 us
    unnamed x12, local copies, waits for them, and re-layouts  7.85 us
  transfers between devices with their start and end apart: 4, of which 4 were waited for; matrix products, arithmetic and copies ran while one was open for 10% of the time, Pallas kernels for 0%

commit v1 on v0

v1 whole, which is shorter than its diff:
```python
import functools

import jax
import jax.numpy as jnp
from jax import lax
from jax.experimental import pallas as pl
from jax.experimental.pallas import tpu as pltpu
from jax.sharding import PartitionSpec as P

MESH = pl.DeviceIdType.MESH
F32, BF16 = jnp.float32, jnp.bfloat16

NX, NY, NZ = 4, 4, 8
PIECE = 48
SHARD = 24
DM = 2304
HALF = DM // 2
FD = 384
CHUNKS = 4
PER = 4
ROWS = PIECE * PER
BLK = ROWS // NZ

XR, XL, YU, YD = (1, 0), (-1, 0), (0, 1), (0, -1)

GATHER = (
    ((1, 0), XR), ((-1, 0), XL), ((0, 1), YU), ((0, -1), YD),
    ((2, 0), XR), ((-1, -1), XL), ((0, 2), YU), ((1, -1), YD),
    ((1, 1), XR), ((2, -1), XL), ((-1, 1), YU), ((-1, 2), YD),
    ((1, 2), XR), ((2, 1), XL), ((2, 2), YD),
)
REDUCE = {
    (1, 0): XR, (2, 0): XR, (1, -1): XR, (1, 1): XR,
    (-1, 0): XL, (-1, -1): XL, (-1, 2): XL,
    (0, 1): YU, (0, 2): YU, (2, 1): YU, (-1, 1): YU,
    (0, -1): YD, (2, 2): YD, (2, -1): YD, (1, 2): YD,
}
CHUNK_PIECES = (
    ((0, 0), (1, 0), (-1, 0), (0, 1)),
    ((2, 0), (-1, -1), (0, 2), (1, -1)),
    ((2, 1), (2, 2), (1, 2), (2, -1)),
    ((0, -1), (1, 1), (-1, 1), (-1, 2)),
)
SLOT = {p: i for i, p in enumerate(p for chunk in CHUNK_PIECES for p in chunk)}


def less(p, d):
    return tuple((a - b + 1) % 4 - 1 for a, b in zip(p, d))


SOURCE = {p: less(p, d) for p, d in GATHER}
PARENT = {p: less(p, d) for p, d in REDUCE.items()}
CHILDREN = {p: [q for q in REDUCE if PARENT[q] == p] for p in SLOT}
NT = (((1,), (1,)), ((), ()))
TN = (((0,), (0,)), ((), ()))


def dot(a, b, dims=(((1,), (0,)), ((), ()))):
    return lax.dot_general(a, b, dims, preferred_element_type=F32)


def kernel(
    x_hbm, wg_hbm, wu_hbm, wd_hbm, c_hbm,
    gi_hbm, gg_hbm, gu_hbm, gd_hbm,
    own, stage, xc, wcat, wd, part, rs_s, rs_r, agb, act,
    gi_own, gi_s, gi_r, tr_s, tr_r, fin, acc_gu, acc_d, out_gu, out_d,
    load_sem, stage_sem, ag_ss, ag_rs, sib_ss, sib_rs, rs_ss, rs_rs, za_ss, za_rs,
    gx_ss, gx_rs, tr_ss, tr_rs, fin_sem, out_sem,
):
    z = lax.axis_index("mp")
    h = lax.axis_index("hidden")
    c = lax.rem(h, 2)
    chip = h // 2
    x, y = lax.rem(chip, NX), chip // NX

    def at(d):
        nx, ny = lax.rem(x + d[0] + NX, NX), lax.rem(y + d[1] + NY, NY)
        return {"hidden": (ny * NX + nx) * 2 + c}

    sibling = {"hidden": h + 1 - 2 * c}

    def zat(o):
        return lax.rem(z + o + 2 * NZ, NZ)

    def send(src, dst, ss, rs, dev):
        return pltpu.make_async_remote_copy(
            src_ref=src, dst_ref=dst, send_sem=ss, recv_sem=rs, device_id=dev, device_id_type=MESH
        )

    sent = []

    def start(copy):
        copy.start()
        sent.append(copy)

    loads = [
        pltpu.make_async_copy(x_hbm, own.at[0], load_sem.at[0]),
        pltpu.make_async_copy(c_hbm, own.at[1], load_sem.at[1]),
        pltpu.make_async_copy(wg_hbm, wcat.at[:, pl.ds(0, FD)], load_sem.at[2]),
        pltpu.make_async_copy(wu_hbm, wcat.at[:, pl.ds(FD, FD)], load_sem.at[3]),
        pltpu.make_async_copy(wd_hbm, wd, load_sem.at[4]),
    ]
    for copy in loads:
        copy.start()

    barrier = pltpu.get_barrier_semaphore()
    for dev in (at(XR), at(XL), at(YU), at(YD), {"mp": zat(1)}, {"mp": zat(-1)}, sibling):
        pl.semaphore_signal(barrier, inc=1, device_id=dev, device_id_type=MESH)
    pl.semaphore_wait(barrier, 7)

    loads[0].wait()
    loads[1].wait()
    swap = send(own.at[1 - c], stage, stage_sem.at[0], stage_sem.at[1], sibling)
    start(swap)
    swap.wait_recv()
    mine, other = own[c].astype(F32), stage[...].astype(F32)
    first = c == 0
    xc[c, SLOT[0, 0]] = jnp.concatenate(
        [jnp.where(first, mine, other), jnp.where(first, other, mine)], axis=0
    ).astype(BF16)

    def share(p):
        s = SLOT[p]
        return send(xc.at[c, s], xc.at[c, s], sib_ss.at[s], sib_rs.at[s], sibling)

    def hop(p, d):
        s = SLOT[p]
        return send(
            xc.at[c, SLOT[SOURCE[p]]], xc.at[c, s], ag_ss.at[s], ag_rs.at[s], at((-d[0], -d[1]))
        )

    def forward(q):
        for p, d in GATHER:
            if SOURCE[p] == q:
                start(hop(p, d))

    def arrive(p, d):
        hop(p, d).wait_recv()
        forward(p)
        start(share(p))

    def gather_step(t):
        for p, d in GATHER[4 * t : 4 * t + 4]:
            arrive(p, d)

    forward((0, 0))
    start(share((0, 0)))

    def rows_of(a, k):
        return xc[a, pl.ds(PER * k, PER)].reshape(ROWS, DM)

    def products(k):
        for p in CHUNK_PIECES[k]:
            s = SLOT[p]
            send(xc.at[1 - c, s], xc.at[1 - c, s], sib_ss.at[s], sib_rs.at[s], sibling).wait_recv()

        def tile(n, _):
            cols = pl.ds(pl.multiple_of(n * 256, 256), 256)
            part[k, :, :, cols] = dot(rows_of(0, k), wcat[:, cols]).reshape(NZ, BLK, 256)
            return 0

        lax.fori_loop(0, 3, tile, 0)
        part[k, :, :, pl.ds(2 * FD, FD)] = dot(rows_of(1, k), wd[...], NT).reshape(NZ, BLK, FD)

    def sign(k):
        return 1 if k % 2 == 0 else -1

    def rs_copy(k, m):
        to = sign(k) if m < 4 else -sign(k)
        return send(rs_s.at[k, m], rs_r.at[k, m], rs_ss.at[k, m], rs_rs.at[k, m], {"mp": zat(to)})

    def rs_send(k, m):
        owner = sign(k) * (4 - m) if m < 4 else -sign(k) * (7 - m)
        value = part[k, zat(owner)]
        if m not in (0, 4):
            rs_copy(k, m - 1).wait_recv()
            value = value + rs_r[k, m - 1].astype(F32)
        rs_s[k, m] = value.astype(BF16)
        start(rs_copy(k, m))

    def za_copy(k, m):
        to = -sign(k) if m < 4 else sign(k)
        hops = m if m < 4 else m - 4
        block = agb.at[k, zat(-to * hops)]
        return send(block, block, za_ss.at[k, m], za_rs.at[k, m], {"mp": zat(to)})

    def za_wait(k, m):
        to = -sign(k) if m < 4 else sign(k)
        hops = m if m < 4 else m - 4
        block = agb.at[k, zat(-to * (hops + 1))]
        send(block, block, za_ss.at[k, m], za_rs.at[k, m], {"mp": zat(to)}).wait_recv()

    def activate(k):
        rs_copy(k, 3).wait_recv()
        rs_copy(k, 6).wait_recv()
        total = part[k, z] + rs_r[k, 3].astype(F32) + rs_r[k, 6].astype(F32)
        gate, up, dhid = total[:, :FD], total[:, FD : 2 * FD], total[:, 2 * FD :]
        sig = jax.nn.sigmoid(gate)
        agb[k, z] = jnp.concatenate(
            [
                gate * sig * up,
                dhid * up * sig * (1.0 + gate * (1.0 - sig)),
                dhid * gate * sig,
            ],
            axis=1,
        ).astype(BF16)
        start(za_copy(k, 0))
        start(za_copy(k, 4))

    def z_step(k, i):
        if i < 4:
            rs_send(k, i)
            if i < 3:
                rs_send(k, 4 + i)
        elif i == 4:
            activate(k)
        elif i < 8:
            za_wait(k, i - 5)
            start(za_copy(k, i - 4))
            za_wait(k, i - 1)
            if i < 7:
                start(za_copy(k, i))
        else:
            za_wait(k, 3)
            act[k] = jnp.concatenate([agb[k, j].astype(F32) for j in range(NZ)], axis=0).astype(BF16)

    def gi_swap(k):
        s = pl.ds(PER * k, PER)
        return send(gi_s.at[s], gi_r.at[s], gx_ss.at[k], gx_rs.at[k], sibling)

    def input_grad(k):
        slots = pl.ds(PER * k, PER)

        def tile(n, half, dst):
            rows = pl.ds(pl.multiple_of(half * HALF + n * FD, 128), FD)
            cols = pl.ds(pl.multiple_of(n * FD, 128), FD)
            value = dot(act[k, :, pl.ds(FD, 2 * FD)], wcat[rows, :], NT)
            dst[slots, :, cols] = value.reshape(PER, PIECE, FD).astype(dst.dtype)
            return 0

        lax.fori_loop(0, 3, lambda n, _: tile(n, 1 - c, gi_s), 0)
        start(gi_swap(k))
        lax.fori_loop(0, 3, lambda n, _: tile(n, c, gi_own), 0)

    def tr_copy(p):
        s = SLOT[p]
        return send(tr_s.at[s], tr_r.at[s], tr_ss.at[s], tr_rs.at[s], at(REDUCE[p]))

    def tree_sum(p):
        s = SLOT[p]
        value = gi_own[s] + gi_r[s].astype(F32)
        for q in CHILDREN[p]:
            tr_copy(q).wait_recv()
            value = value + tr_r[SLOT[q]].astype(F32)
        return value

    def tree(*pieces):
        for p in pieces:
            tr_s[SLOT[p]] = tree_sum(p).astype(BF16)
            start(tr_copy(p))

    outs = []

    def weight_grads(k):
        last = k == CHUNKS - 1
        slots = pl.ds(PER * k, PER)

        def gu_tile(n, _):
            cols = pl.ds(pl.multiple_of(n * 256, 256), 256)
            value = dot(xc[0, slots, :, cols].reshape(ROWS, 256), act[k, :, pl.ds(FD, 2 * FD)], TN)
            if k:
                value = value + acc_gu[cols, :]
            if last:
                out_gu[cols, :] = value.astype(BF16)
            else:
                acc_gu[cols, :] = value
            return 0

        def d_tile(n, _):
            cols = pl.ds(pl.multiple_of(n * 256, 256), 256)
            value = dot(act[k, :, pl.ds(0, FD)], xc[1, slots, :, cols].reshape(ROWS, 256), TN)
            if k:
                value = value + acc_d[:, cols]
            if last:
                out_d[:, cols] = value.astype(BF16)
            else:
                acc_d[:, cols] = value
            return 0

        lax.fori_loop(0, DM // 256, gu_tile, 0)
        if last:
            outs.append(pltpu.make_async_copy(out_gu.at[:, pl.ds(0, FD)], gg_hbm, out_sem.at[0]))
            outs.append(pltpu.make_async_copy(out_gu.at[:, pl.ds(FD, FD)], gu_hbm, out_sem.at[1]))
            outs[0].start()
            outs[1].start()
        lax.fori_loop(0, DM // 256, d_tile, 0)
        if last:
            outs.append(pltpu.make_async_copy(out_d, gd_hbm, out_sem.at[2]))
            outs[2].start()

    gather_step(0)
    for copy in loads[2:]:
        copy.wait()
    products(0)
    z_step(0, 0)
    gather_step(1)
    z_step(0, 1)
    products(1)
    z_step(0, 2)
    z_step(1, 0)
    gather_step(2)
    z_step(0, 3)
    z_step(1, 1)
    gather_step(3)
    z_step(0, 4)
    z_step(1, 2)
    products(2)
    z_step(0, 5)
    z_step(1, 3)
    z_step(2, 0)
    products(3)
    z_step(0, 6)
    z_step(1, 4)
    z_step(2, 1)
    z_step(3, 0)
    z_step(0, 7)
    z_step(1, 5)
    z_step(2, 2)
    z_step(3, 1)
    z_step(0, 8)
    input_grad(0)
    z_step(1, 6)
    z_step(2, 3)
    z_step(3, 2)
    weight_grads(0)
    z_step(1, 7)
    z_step(2, 4)
    z_step(3, 3)
    gi_swap(0).wait_recv()
    z_step(1, 8)
    input_grad(1)
    z_step(2, 5)
    z_step(3, 4)
    gi_swap(1).wait_recv()
    tree((-1, -1))
    z_step(2, 6)
    z_step(3, 5)
    weight_grads(1)
    z_step(2, 7)
    z_step(3, 6)
    z_step(2, 8)
    input_grad(2)
    z_step(3, 7)
    gi_swap(2).wait_recv()
    tree((2, 2), (2, 1), (1, 2))
    z_step(3, 8)
    input_grad(3)
    tree((2, -1), (1, -1))
    gi_swap(3).wait_recv()
    tree((1, 1), (-1, 1), (-1, 2))
    tree((2, 0), (0, -1))
    weight_grads(2)
    tree((1, 0), (-1, 0), (0, 2))
    tree((0, 1))
    weight_grads(3)

    gi_own[SLOT[0, 0]] = tree_sum((0, 0))
    theirs = pl.ds(pl.multiple_of((1 - c) * SHARD, 8), SHARD)
    ours = pl.ds(pl.multiple_of(c * SHARD, 8), SHARD)
    fin[2] = gi_own[SLOT[0, 0], theirs, :].astype(BF16)
    last = send(fin.at[2], fin.at[1], fin_sem.at[0], fin_sem.at[1], sibling)
    start(last)
    fin[0] = gi_own[SLOT[0, 0], ours, :].astype(BF16)
    half_c = pl.ds(pl.multiple_of(c * HALF, 128), HALF)
    half_o = pl.ds(pl.multiple_of((1 - c) * HALF, 128), HALF)
    outs.append(pltpu.make_async_copy(fin.at[0], gi_hbm.at[:, half_c], out_sem.at[3]))
    outs[3].start()
    last.wait_recv()
    outs.append(pltpu.make_async_copy(fin.at[1], gi_hbm.at[:, half_o], out_sem.at[4]))
    outs[4].start()

    for copy in outs:
        copy.wait()
    for copy in sent:
        copy.wait_send()


def shards(inputs, gate_weight, up_weight, down_weight, cotangent):
    dma = pltpu.SemaphoreType.DMA
    any_spec = pl.BlockSpec(memory_space=pl.ANY)
    slots = CHUNKS * PER
    return pl.pallas_call(
        kernel,
        out_shape=(
            jax.ShapeDtypeStruct((SHARD, DM), BF16),
            jax.ShapeDtypeStruct((DM, FD), BF16),
            jax.ShapeDtypeStruct((DM, FD), BF16),
            jax.ShapeDtypeStruct((FD, DM), BF16),
        ),
        in_specs=[any_spec] * 5,
        out_specs=(any_spec,) * 4,
        scratch_shapes=[
            pltpu.VMEM((2, SHARD, DM), BF16),
            pltpu.VMEM((SHARD, DM), BF16),
            pltpu.VMEM((2, slots, PIECE, DM), BF16),
            pltpu.VMEM((DM, 2 * FD), BF16),
            pltpu.VMEM((FD, DM), BF16),
            pltpu.VMEM((CHUNKS, NZ, BLK, 3 * FD), F32),
            pltpu.VMEM((CHUNKS, 7, BLK, 3 * FD), BF16),
            pltpu.VMEM((CHUNKS, 7, BLK, 3 * FD), BF16),
            pltpu.VMEM((CHUNKS, NZ, BLK, 3 * FD), BF16),
            pltpu.VMEM((CHUNKS, ROWS, 3 * FD), BF16),
            pltpu.VMEM((slots, PIECE, HALF), F32),
            pltpu.VMEM((slots, PIECE, HALF), BF16),
            pltpu.VMEM((slots, PIECE, HALF), BF16),
            pltpu.VMEM((slots, PIECE, HALF), BF16),
            pltpu.VMEM((slots, PIECE, HALF), BF16),
            pltpu.VMEM((3, SHARD, HALF), BF16),
            pltpu.VMEM((DM, 2 * FD), F32),
            pltpu.VMEM((FD, DM), F32),
            pltpu.VMEM((DM, 2 * FD), BF16),
            pltpu.VMEM((FD, DM), BF16),
            dma((5,)),
            dma((2,)),
            dma((slots,)), dma((slots,)),
            dma((slots,)), dma((slots,)),
            dma((CHUNKS, 7)), dma((CHUNKS, 7)),
            dma((CHUNKS, 7)), dma((CHUNKS, 7)),
            dma((CHUNKS,)), dma((CHUNKS,)),
            dma((slots,)), dma((slots,)),
            dma((2,)),
            dma((5,)),
        ],
        compiler_params=pltpu.CompilerParams(
            collective_id=0, has_side_effects=True, vmem_limit_bytes=60 * 1024 * 1024
        ),
    )(inputs, gate_weight, up_weight, down_weight, cotangent)


def solution(mesh):
    placed = (
        P("hidden", "mp"),
        P("mp", "hidden"),
        P("mp", "hidden"),
        P("hidden", "mp"),
        P("hidden", "mp"),
    )
    return jax.shard_map(
        shards,
        mesh=mesh,
        in_specs=placed,
        out_specs=(P("hidden", "mp"), P("mp", "hidden"), P("mp", "hidden"), P("hidden", "mp")),
        check_vma=False,
    )
```

time: 322 us -> 128 us (0.40)
  waiting for transfers between devices: 262 us -> 0 us
  Pallas kernels: 0 us -> 119 us
  matrix products: 34.7 us -> 0 us
  between operations: 13.8 us -> 0.64 us
    pallas_call x0 -> x1, Pallas kernels: none -> 119 us  [shards(): pl.pallas_call(kernel, out_shape=(jax.ShapeDtypeStruct((SHARD, DM), BF16)...]
    all_gather x2 -> x0, waiting for transfers between devices: 101 us -> none  [the longest x1 56.8 us: shards(): rows_in = lax.all_gather(inputs, 'hidden', axis=0, tiled=True)]
    psum x1 -> x0, waiting for transfers between devices: 97.1 us -> none  [shards(): gate, up, dhid = lax.psum((gate_term, up_term, down_term), 'mp')]
    reduce_scatter x1 -> x0, waiting for transfers between devices: 62.6 us -> none  [shards(): lax.psum_scatter((first + second).astype(jnp.bfloat16), 'hidden', scatter...]
    dot_general x8 -> x0, matrix products: 34.7 us -> none  [the longest x1 5.57 us: shards(): lax.dot_general(rows_cot, down_weight, (((1,), (1,)), ((), ())), preferre...]
    unnamed x12 -> x8, local copies, waits for them, and re-layouts: 7.85 us -> 7.86 us
  transfers between devices with their start and end apart: 4 -> 0, of which waited for: 4 -> 0; matrix products, arithmetic and copies ran while one was open for 10% -> 0% of each run, Pallas kernels for 0% -> 0%
where the time goes in v1:
time: 128 us
  Pallas kernels  119 us (93%)
  local copies, waits for them, and re-layouts  7.86 us (6%)
    pallas_call x1, Pallas kernels, shards(): pl.pallas_call(kernel, out_shape=(jax.ShapeDtypeStruct((SHARD, DM), BF16)...  119 us
    unnamed x8, local copies, waits for them, and re-layouts  7.86 us

profile of v1, /device:TPU:1, one launch (start us, length us, event | category | flops | bytes accessed | tf_op | source)
XLA Modules:
  0.0 127.6 jit_solution(6649252638171087701)
XLA Ops:
  0.6 119.1 %shard_map.84 = (bf16[24,2304]{1,0:T(8,128)(2,1)}, bf16[2304,384]{1,0:T(8,128)(2,1)}, bf16[2304,384]{1,0:T(8,128)(2,1)}, bf16[384,2304]{1,0:T(8,128)(2,1)}) custom-call(bf16[24,2304]{1,0:T(8,128)(2,1)} %x_hbm.1, bf16[2304,384]{1,0:T(8,128)(2,1)} %wg_hbm.1, bf16[2304,384]{1,0:T(8,128)(2,1)} %wu_hbm.1, bf16[384,2304]{1,0:T(8,128)(2,1)} %wd_hbm.1, ...), custom_call_target="tpu_custom_call" | custom-call | tf_op jit(solution)/shard_map/pallas_call | solution.py:392
  119.8 1.5 %copy.13 = bf16[24,2304]{1,0:T(8,128)(2,1)} copy(bf16[24,2304]{1,0:T(8,128)(2,1)} %get-tuple-element.8) | data formatting | bytes 221184
  121.3 0.0 copy-start.1
  121.3 3.0 %copy.14 = bf16[2304,384]{1,0:T(8,128)(2,1)} copy(bf16[2304,384]{1,0:T(8,128)(2,1)} %get-tuple-element.9) | data formatting | bytes 3538944
  124.3 0.0 copy-done.1
  124.3 0.0 copy-start
  124.3 1.2 copy.15
  125.5 0.9 copy-done
  126.4 1.2 copy.16
Async XLA Ops:
  121.3 3.0 %copy-start.1 = (bf16[2304,384]{1,0:T(8,128)(2,1)S(1)}, bf16[2304,384]{1,0:T(8,128)(2,1)}, u32[]{:S(2)}) copy-start(bf16[2304,384]{1,0:T(8,128)(2,1)} %get-tuple-element.10) | copy-start | bytes 5308420
  124.3 2.1 %copy-start = (bf16[384,2304]{1,0:T(8,128)(2,1)S(1)}, bf16[384,2304]{1,0:T(8,128)(2,1)}, u32[]{:S(2)}) copy-start(bf16[384,2304]{1,0:T(8,128)(2,1)} %get-tuple-element.11) | copy-start | bytes 5308420

commit v2 on v0

v2 whole, which is shorter than its diff:
```python
import functools

import jax
import jax.numpy as jnp
from jax import lax
from jax.experimental import pallas as pl
from jax.experimental.pallas import tpu as pltpu
from jax.sharding import PartitionSpec as P

MESH = pl.DeviceIdType.MESH
F32, BF16 = jnp.float32, jnp.bfloat16

NX, NY, NZ = 4, 4, 8
PIECE = 48
SHARD = 24
DM = 2304
HALF = DM // 2
FD = 384
CHUNKS = 4
PER = 4
ROWS = PIECE * PER
BLK = ROWS // NZ

XR, XL, YU, YD = (1, 0), (-1, 0), (0, 1), (0, -1)

GATHER = (
    ((1, 0), (1, 0)),
    ((-1, 0), (-1, 0)),
    ((0, 1), (0, 1)),
    ((0, -1), (0, -1)),
    ((2, 0), (1, 0)),
    ((-1, -1), (-1, 0)),
    ((0, 2), (0, 1)),
    ((1, -1), (0, -1)),
    ((1, 1), (1, 0)),
    ((2, -1), (-1, 0)),
    ((-1, 1), (0, 1)),
    ((-1, 2), (0, -1)),
    ((1, 2), (1, 0)),
    ((2, 1), (-1, 0)),
    ((2, 2), (0, -1)),
)
REDUCE = {
    (1, 0): (1, 0),
    (-1, 0): (-1, 0),
    (0, 1): (0, 1),
    (0, -1): (0, -1),
    (1, 1): (1, 1),
    (-1, 1): (-1, 1),
    (1, -1): (1, -1),
    (-1, -1): (-1, -1),
    (2, 0): (1, 0),
    (0, 2): (0, 1),
    (2, 1): (-1, 0),
    (2, -1): (1, 0),
    (1, 2): (0, -1),
    (-1, 2): (0, 1),
    (2, 2): (-1, -1),
}
CHUNK_PIECES = (
    ((0, 0), (1, 0), (-1, 0), (0, 1)),
    ((2, 0), (-1, -1), (0, 2), (1, -1)),
    ((2, 1), (2, 2), (1, 2), (2, -1)),
    ((0, -1), (1, 1), (-1, 1), (-1, 2)),
)
RING = {1: 1, 2: 1, 3: 1, 4: 1, -1: -1, -2: -1, -3: -1}
SHORT = {1: 1, 2: 2, 3: 1, 4: 2, -1: -1, -2: -1, -3: -2}
SUM_TREE = (RING, RING, RING, RING)
SPREAD_TREE = (RING, RING, RING, RING)
ORDER = (
    ("Y",), ("G", 1, 0), ("G", 3, 0), ("G", 2, 0), ("G", 12, 0),
    ("G", 1, 1), ("G", 3, 1), ("G", 2, 1), ("G", 12, 1), ("F", 0, 0),
    ("G", 7, 0), ("G", 4, 0), ("G", 6, 0), ("G", 5, 0), ("F", 0, 3),
    ("R", 0, -3), ("R", 0, 4), ("X", 0), ("G", 14, 0), ("G", 7, 1),
    ("G", 13, 0), ("G", 5, 1), ("G", 4, 1), ("G", 6, 1), ("R", 0, -2),
    ("G", 15, 0), ("G", 11, 0), ("R", 0, 3), ("F", 1, 0), ("G", 13, 1),
    ("G", 14, 1), ("F", 1, 3), ("G", 8, 0), ("G", 15, 1), ("R", 1, 4),
    ("R", 1, -3), ("R", 0, -1), ("X", 1), ("G", 10, 0), ("G", 11, 1),
    ("R", 0, 2), ("G", 9, 0), ("F", 3, 0), ("G", 10, 1), ("F", 3, 3),
    ("G", 8, 1), ("R", 1, -2), ("R", 1, 3), ("R", 3, -3), ("R", 3, 4),
    ("X", 3), ("R", 0, 1), ("G", 9, 1), ("F", 2, 0), ("R", 1, -1),
    ("R", 1, 2), ("F", 2, 3), ("R", 2, 4), ("R", 3, -2), ("R", 2, -3),
    ("A", 0), ("R", 3, 3), ("X", 2), ("R", 1, 1), ("R", 2, 3),
    ("R", 2, -2), ("R", 3, -1), ("Z", 0, -1), ("Z", 0, 1), ("R", 3, 2),
    ("R", 2, 2), ("A", 1), ("R", 2, -1), ("Z", 0, 2), ("Z", 0, -2),
    ("R", 2, 1), ("R", 3, 1), ("Z", 1, -1), ("Z", 1, 1), ("Z", 0, 3),
    ("A", 2), ("Z", 0, -3), ("Z", 1, -2), ("A", 3), ("Z", 0, 4),
    ("C", 0), ("Z", 1, 2), ("S", 0), ("W", 0, 0), ("Z", 2, 1),
    ("Z", 2, -1), ("W", 0, 1), ("W", 0, 2), ("Z", 1, -3), ("Z", 3, 1),
    ("O", 0), ("Z", 3, -1), ("Z", 1, 3), ("T", 2), ("W", 0, 3),
    ("W", 0, 4), ("Z", 2, 2), ("Z", 2, -2), ("W", 0, 5), ("Z", 3, 2),
    ("Z", 3, -2), ("Z", 1, 4), ("C", 1), ("S", 1), ("Z", 2, 3),
    ("Z", 2, -3), ("W", 1, 0), ("W", 1, 1), ("Z", 3, 3), ("W", 1, 2),
    ("O", 1), ("Z", 3, -3), ("T", 4), ("T", 6), ("W", 1, 3),
    ("Z", 2, 4), ("C", 2), ("S", 2), ("Z", 3, 4), ("C", 3),
    ("S", 3), ("W", 1, 4), ("O", 2), ("T", 9), ("T", 10),
    ("T", 8), ("T", 3), ("T", 11), ("T", 1), ("O", 3),
    ("T", 12), ("T", 15), ("T", 13), ("W", 1, 5), ("W", 2, 0),
    ("W", 2, 1), ("W", 2, 2), ("W", 2, 3), ("W", 2, 4), ("W", 2, 5),
    ("W", 3, 0), ("W", 3, 1), ("W", 3, 2), ("T", 5), ("T", 14),
    ("W", 3, 3), ("W", 3, 4), ("W", 3, 5), ("T", 7), ("E",),
)
SLOT = {p: i for i, p in enumerate(p for chunk in CHUNK_PIECES for p in chunk)}
OWN = SLOT[0, 0]


def less(p, d):
    return tuple((a - b + 1) % 4 - 1 for a, b in zip(p, d))


SOURCE = {p: less(p, d) for p, d in GATHER}
COMES = dict(GATHER)
PARENT = {p: less(p, d) for p, d in REDUCE.items()}
CHILDREN = {p: [q for q in REDUCE if PARENT[q] == p] for p in SLOT}
PIECES = {s: p for p, s in SLOT.items()}
OFFSETS = tuple(RING)
NT = (((1,), (1,)), ((), ()))
W_ORDER = [step[1] for step in ORDER if step[0] == "W" and step[2] == 0]


def dot(a, b, dims=(((1,), (0,)), ((), ()))):
    return lax.dot_general(a, b, dims, preferred_element_type=F32)


def kernel(
    x_hbm, wg_hbm, wu_hbm, wd_hbm, c_hbm,
    gi_out, gg_out, gu_out, gd_out,
    own, stage, xc, xt, wcat, wt, wd, part, rs_s, rs_r, agb, act, ht,
    gi_own, gi_s, gi_r, tr_s, tr_r, fin, acc_gu, acc_d,
    load_sem, stage_sem, ag_ss, ag_rs, sib_ss, sib_rs, rs_ss, rs_rs, za_ss, za_rs,
    gx_ss, gx_rs, tr_ss, tr_rs, fin_sem,
):
    z = lax.axis_index("mp")
    h = lax.axis_index("hidden")
    c = lax.rem(h, 2)
    chip = h // 2
    x, y = lax.rem(chip, NX), chip // NX

    def at(d):
        nx, ny = lax.rem(x + d[0] + NX, NX), lax.rem(y + d[1] + NY, NY)
        return {"hidden": (ny * NX + nx) * 2 + c}

    sibling = {"hidden": h + 1 - 2 * c}

    def zat(o):
        return lax.rem(z + o + NZ, NZ)

    def send(src, dst, ss, rs, dev):
        return pltpu.make_async_remote_copy(
            src_ref=src, dst_ref=dst, send_sem=ss, recv_sem=rs, device_id=dev, device_id_type=MESH
        )

    sent = []

    def start(copy):
        copy.start()
        sent.append(copy)

    loads = [
        pltpu.make_async_copy(x_hbm, own.at[0], load_sem.at[0]),
        pltpu.make_async_copy(c_hbm, own.at[1], load_sem.at[1]),
        pltpu.make_async_copy(wg_hbm, wcat.at[:, pl.ds(0, FD)], load_sem.at[2]),
        pltpu.make_async_copy(wu_hbm, wcat.at[:, pl.ds(FD, FD)], load_sem.at[3]),
        pltpu.make_async_copy(wd_hbm, wd, load_sem.at[4]),
    ]
    for copy in loads:
        copy.start()

    reach = sorted({d for d in COMES.values()} | {(-a, -b) for a, b in COMES.values()}
                   | set(REDUCE.values()) | {(-a, -b) for a, b in REDUCE.values()})
    reach = sorted({((a + 1) % 4 - 1, (b + 1) % 4 - 1) for a, b in reach})
    along = sorted({s * d for tree in SUM_TREE + SPREAD_TREE for d in tree.values() for s in (1, -1)})
    greet = [at(d) for d in reach] + [{"mp": zat(d)} for d in along] + [sibling]
    barrier = pltpu.get_barrier_semaphore()
    for dev in greet:
        pl.semaphore_signal(barrier, inc=1, device_id=dev, device_id_type=MESH)
    pl.semaphore_wait(barrier, len(greet))

    loads[0].wait()
    loads[1].wait()
    swap = send(own.at[1 - c], stage, stage_sem.at[0], stage_sem.at[1], sibling)
    start(swap)
    swap.wait_recv()
    mine, other = own[c].astype(F32), stage[...].astype(F32)
    first = c == 0
    xc[c, OWN] = jnp.concatenate(
        [jnp.where(first, mine, other), jnp.where(first, other, mine)], axis=0
    ).astype(BF16)

    def share(a, s, half):
        part_of = xc.at[a, s, :, pl.ds(half * HALF, HALF)]
        return send(part_of, part_of, sib_ss.at[s, half], sib_rs.at[s, half], sibling)

    def hop(p, half):
        s, d, cols = SLOT[p], COMES[p], pl.ds(half * HALF, HALF)
        return send(
            xc.at[c, SLOT[SOURCE[p]], :, cols], xc.at[c, s, :, cols],
            ag_ss.at[s, half], ag_rs.at[s, half], at((-d[0], -d[1])),
        )

    def forward(q, half):
        for p, _ in GATHER:
            if SOURCE[p] == q:
                start(hop(p, half))

    def gather(s, half):
        hop(PIECES[s], half).wait_recv()
        forward(PIECES[s], half)
        start(share(c, s, half))

    for half in (0, 1):
        forward((0, 0), half)
    for half in (0, 1):
        start(share(c, OWN, half))

    def flip_weights():
        for copy in loads[2:]:
            copy.wait()

        def tile(n, _):
            cols = pl.ds(pl.multiple_of(n * 256, 256), 256)
            wt[:, cols] = wcat[cols, :].T
            return 0

        lax.fori_loop(0, DM // 256, tile, 0)

    def flip_inputs(k):
        def tile(n, _):
            cols = pl.ds(pl.multiple_of(n * 256, 256), 256)
            xt[k, cols, pl.ds(0, ROWS)] = xc[0, pl.ds(PER * k, PER), :, cols].reshape(ROWS, 256).T
            return 0

        lax.fori_loop(0, DM // 256, tile, 0)

    def rows_of(a, k):
        return xc[a, pl.ds(PER * k, PER)].reshape(ROWS, DM)

    def product(k, n):
        if n == 0:
            for i in range(PER * k, PER * k + PER):
                for half in (0, 1):
                    share(1 - c, i, half).wait_recv()
            part[k, :, :, pl.ds(0, 2 * FD)] = dot(rows_of(0, k), wcat[...]).reshape(NZ, BLK, 2 * FD)
        else:
            part[k, :, :, pl.ds(2 * FD, FD)] = dot(rows_of(1, k), wd[...], NT).reshape(NZ, BLK, FD)

    def sign(k):
        return 1 if k % 2 == 0 else -1

    def sum_copy(k, o):
        m = OFFSETS.index(o)
        dev = {"mp": zat(sign(k) * SUM_TREE[k][o])}
        return send(rs_s.at[k, m], rs_r.at[k, m], rs_ss.at[k, m], rs_rs.at[k, m], dev)

    def sum_at(k, o):
        value = part[k, zat(sign(k) * o)]
        for q, d in SUM_TREE[k].items():
            if q - d == o:
                sum_copy(k, q).wait_recv()
                value = value + rs_r[k, OFFSETS.index(q)].astype(F32)
        return value

    def reduce(k, o):
        rs_s[k, OFFSETS.index(o)] = sum_at(k, o).astype(BF16)
        start(sum_copy(k, o))

    def spread_copy(k, o):
        m, d = OFFSETS.index(o), SPREAD_TREE[k][o]
        block = agb.at[k, zat(-sign(k) * (o - d))]
        return send(block, block, za_ss.at[k, m], za_rs.at[k, m], {"mp": zat(sign(k) * d)})

    def spread_wait(k, o):
        m, d = OFFSETS.index(o), SPREAD_TREE[k][o]
        block = agb.at[k, zat(-sign(k) * o)]
        send(block, block, za_ss.at[k, m], za_rs.at[k, m], {"mp": zat(sign(k) * d)}).wait_recv()

    def spread_on(k, q):
        for o, d in SPREAD_TREE[k].items():
            if o - d == q:
                start(spread_copy(k, o))

    def spread(k, o):
        spread_wait(k, o)
        spread_on(k, o)

    def activate(k):
        total = sum_at(k, 0)
        gate, up, dhid = total[:, :FD], total[:, FD : 2 * FD], total[:, 2 * FD :]
        sig = jax.nn.sigmoid(gate)
        agb[k, z] = jnp.concatenate(
            [
                gate * sig * up,
                dhid * up * sig * (1.0 + gate * (1.0 - sig)),
                dhid * gate * sig,
            ],
            axis=1,
        ).astype(BF16)
        spread_on(k, 0)

    def collect(k):
        act[k] = jnp.concatenate([agb[k, j].astype(F32) for j in range(NZ)], axis=0).astype(BF16)
        ht[k, :, pl.ds(0, ROWS)] = act[k, :, pl.ds(0, FD)].T

    def gi_swap(k):
        s = pl.ds(PER * k, PER)
        return send(gi_s.at[s], gi_r.at[s], gx_ss.at[k], gx_rs.at[k], sibling)

    def input_grad(k, half, dst):
        cols = pl.ds(pl.multiple_of(half * HALF, 128), HALF)
        value = dot(act[k, :, pl.ds(FD, 2 * FD)], wt[:, cols])
        dst[pl.ds(PER * k, PER)] = value.reshape(PER, PIECE, HALF).astype(dst.dtype)

    def their_half(k):
        input_grad(k, 1 - c, gi_s)
        start(gi_swap(k))

    def our_half(k):
        input_grad(k, c, gi_own)
        gi_swap(k).wait_recv()

    def tr_copy(p):
        s = SLOT[p]
        return send(tr_s.at[s], tr_r.at[s], tr_ss.at[s], tr_rs.at[s], at(REDUCE[p]))

    def tree_sum(p):
        s = SLOT[p]
        value = gi_own[s] + gi_r[s].astype(F32)
        for q in CHILDREN[p]:
            tr_copy(q).wait_recv()
            value = value + tr_r[SLOT[q]].astype(F32)
        return value

    def tree(s):
        tr_s[s] = tree_sum(PIECES[s]).astype(BF16)
        start(tr_copy(PIECES[s]))

    def weight_grads(k, i):
        last = k == W_ORDER[-1]
        slots = pl.ds(PER * k, PER)

        cols = pl.ds(DM // 3 * (i % 3), DM // 3)
        if i < 3:
            value = dot(xt[k, cols, pl.ds(0, ROWS)], act[k, :, pl.ds(FD, 2 * FD)])
            if k != W_ORDER[0]:
                value = value + acc_gu[cols, :]
            if last:
                gg_out[cols, :] = value[:, :FD].astype(BF16)
                gu_out[cols, :] = value[:, FD:].astype(BF16)
            else:
                acc_gu[cols, :] = value
        else:
            value = dot(ht[k, :, pl.ds(0, ROWS)], xc[1, slots, :, cols].reshape(ROWS, DM // 3))
            if k != W_ORDER[0]:
                value = value + acc_d[:, cols]
            if last:
                gd_out[:, cols] = value.astype(BF16)
            else:
                acc_d[:, cols] = value

    def finish():
        gi_own[OWN] = tree_sum((0, 0))
        theirs = pl.ds(pl.multiple_of((1 - c) * SHARD, 8), SHARD)
        ours = pl.ds(pl.multiple_of(c * SHARD, 8), SHARD)
        fin[1] = gi_own[OWN, theirs, :].astype(BF16)
        copy = send(fin.at[1], fin.at[0], fin_sem.at[0], fin_sem.at[1], sibling)
        start(copy)
        gi_out[:, pl.ds(pl.multiple_of(c * HALF, 128), HALF)] = gi_own[OWN, ours, :].astype(BF16)
        copy.wait_recv()
        gi_out[:, pl.ds(pl.multiple_of((1 - c) * HALF, 128), HALF)] = fin[0]

    steps = {
        "G": gather, "F": product, "R": reduce, "A": activate, "Z": spread, "C": collect,
        "S": their_half, "O": our_half, "T": tree, "W": weight_grads, "E": finish, "X": flip_inputs, "Y": flip_weights,
    }
    for step, *numbers in ORDER:
        steps[step](*numbers)
    for copy in sent:
        copy.wait_send()


def store(*refs):
    n = len(refs) // 2
    copies = [pltpu.make_async_copy(refs[i], refs[n + i], refs[-1].at[i]) for i in range(n)]
    for copy in copies:
        copy.start()
    for copy in copies:
        copy.wait()


def shards(inputs, gate_weight, up_weight, down_weight, cotangent):
    dma = pltpu.SemaphoreType.DMA
    any_spec = pl.BlockSpec(memory_space=pl.ANY)
    slots, offsets = CHUNKS * PER, len(OFFSETS)
    shapes = ((SHARD, DM), (DM, FD), (DM, FD), (FD, DM))
    results = pl.pallas_call(
        kernel,
        out_shape=tuple(pltpu.VMEM(shape, BF16) for shape in shapes),
        in_specs=[any_spec] * 5,
        out_specs=(pl.BlockSpec(memory_space=pltpu.VMEM),) * 4,
        scratch_shapes=[
            pltpu.VMEM((2, SHARD, DM), BF16),
            pltpu.VMEM((SHARD, DM), BF16),
            pltpu.VMEM((2, slots, PIECE, DM), BF16),
            pltpu.VMEM((CHUNKS, DM, 256), BF16),
            pltpu.VMEM((DM, 2 * FD), BF16),
            pltpu.VMEM((2 * FD, DM), BF16),
            pltpu.VMEM((FD, DM), BF16),
            pltpu.VMEM((CHUNKS, NZ, BLK, 3 * FD), F32),
            pltpu.VMEM((CHUNKS, offsets, BLK, 3 * FD), BF16),
            pltpu.VMEM((CHUNKS, offsets, BLK, 3 * FD), BF16),
            pltpu.VMEM((CHUNKS, NZ, BLK, 3 * FD), BF16),
            pltpu.VMEM((CHUNKS, ROWS, 3 * FD), BF16),
            pltpu.VMEM((CHUNKS, FD, 256), BF16),
            pltpu.VMEM((slots, PIECE, HALF), F32),
            pltpu.VMEM((slots, PIECE, HALF), BF16),
            pltpu.VMEM((slots, PIECE, HALF), BF16),
            pltpu.VMEM((slots, PIECE, HALF), BF16),
            pltpu.VMEM((slots, PIECE, HALF), BF16),
            pltpu.VMEM((2, SHARD, HALF), BF16),
            pltpu.VMEM((DM, 2 * FD), F32),
            pltpu.VMEM((FD, DM), F32),
            dma((5,)),
            dma((2,)),
            dma((slots, 2)), dma((slots, 2)),
            dma((slots, 2)), dma((slots, 2)),
            dma((CHUNKS, offsets)), dma((CHUNKS, offsets)),
            dma((CHUNKS, offsets)), dma((CHUNKS, offsets)),
            dma((CHUNKS,)), dma((CHUNKS,)),
            dma((slots,)), dma((slots,)),
            dma((2,)),
        ],
        compiler_params=pltpu.CompilerParams(
            collective_id=0, has_side_effects=True, vmem_limit_bytes=57 * 1024 * 1024
        ),
    )(inputs, gate_weight, up_weight, down_weight, cotangent)
    return pl.pallas_call(
        store,
        out_shape=tuple(jax.ShapeDtypeStruct(shape, BF16) for shape in shapes),
        in_specs=[pl.BlockSpec(memory_space=pltpu.VMEM)] * 4,
        out_specs=(any_spec,) * 4,
        scratch_shapes=[dma((4,))],
        compiler_params=pltpu.CompilerParams(vmem_limit_bytes=1024 * 1024),
    )(*(pltpu.with_memory_space_constraint(a, pltpu.VMEM) for a in results))


def solution(mesh):
    placed = (
        P("hidden", "mp"),
        P("mp", "hidden"),
        P("mp", "hidden"),
        P("hidden", "mp"),
        P("hidden", "mp"),
    )
    return jax.shard_map(
        shards,
        mesh=mesh,
        in_specs=placed,
        out_specs=(P("hidden", "mp"), P("mp", "hidden"), P("mp", "hidden"), P("hidden", "mp")),
        check_vma=False,
    )
```

time: 322 us -> 92 us (0.29)
  waiting for transfers between devices: 262 us -> 0 us
  Pallas kernels: 0 us -> 91.1 us
  matrix products: 34.7 us -> 0 us
  between operations: 13.8 us -> 0.8 us
  local copies, waits for them, and re-layouts: 7.85 us -> 0 us
    all_gather x2 -> x0, waiting for transfers between devices: 101 us -> none  [the longest x1 56.8 us: shards(): rows_in = lax.all_gather(inputs, 'hidden', axis=0, tiled=True)]
    psum x1 -> x0, waiting for transfers between devices: 97.1 us -> none  [shards(): gate, up, dhid = lax.psum((gate_term, up_term, down_term), 'mp')]
    pallas_call x0 -> x2, Pallas kernels: none -> 91.1 us  [the longest x1 88.7 us: shards(): pl.pallas_call(kernel, out_shape=tuple((pltpu.VMEM(shape, BF16) for shape...]
    reduce_scatter x1 -> x0, waiting for transfers between devices: 62.6 us -> none  [shards(): lax.psum_scatter((first + second).astype(jnp.bfloat16), 'hidden', scatter...]
    dot_general x8 -> x0, matrix products: 34.7 us -> none  [the longest x1 5.57 us: shards(): lax.dot_general(rows_cot, down_weight, (((1,), (1,)), ((), ())), preferre...]
    unnamed x12 -> x0, local copies, waits for them, and re-layouts: 7.85 us -> none
  transfers between devices with their start and end apart: 4 -> 0, of which waited for: 4 -> 0; matrix products, arithmetic and copies ran while one was open for 10% -> 0% of each run, Pallas kernels for 0% -> 0%
where the time goes in v2:
time: 92 us; the launch traced here: 91.9 us
  Pallas kernels  91.1 us (99%)
    pallas_call x1, Pallas kernels, shards(): pl.pallas_call(kernel, out_shape=tuple((pltpu.VMEM(shape, BF16) for shape...  88.7 us
    pallas_call x1, Pallas kernels, shards(): pl.pallas_call(store, out_shape=tuple((jax.ShapeDtypeStruct(shape, BF16)...  2.45 us

profile of v2, /device:TPU:1, one launch (start us, length us, event | category | flops | bytes accessed | tf_op | source)
XLA Modules:
  0.0 91.9 jit_solution(11975066224799932161)
XLA Ops:
  0.6 88.7 %shard_map.84 = (bf16[24,2304]{1,0:T(8,128)(2,1)S(1)}, bf16[2304,384]{1,0:T(8,128)(2,1)S(1)}, bf16[2304,384]{1,0:T(8,128)(2,1)S(1)}, bf16[384,2304]{1,0:T(8,128)(2,1)S(1)}) custom-call(bf16[24,2304]{1,0:T(8,128)(2,1)} %x_hbm.1, bf16[2304,384]{1,0:T(8,128)(2,1)} %wg_hbm.1, bf16[2304,384]{1,0:T(8,128)(2,1)} %wu_hbm.1, bf16[384,2304]{1,0:T(8,128)(2,1)} %wd_hbm.1, ...), custom_call_target="tpu_custom_call" | custom-call | tf_op jit(solution)/shard_map/pallas_call | solution.py:395
  89.3 2.4 %shard_map.85 = (bf16[24,2304]{1,0:T(8,128)(2,1)}, bf16[2304,384]{1,0:T(8,128)(2,1)}, bf16[2304,384]{1,0:T(8,128)(2,1)}, bf16[384,2304]{1,0:T(8,128)(2,1)}) custom-call(bf16[24,2304]{1,0:T(8,128)(2,1)S(1)} %get-tuple-element.8.refs_0_, bf16[2304,384]{1,0:T(8,128)(2,1)S(1)} %get-tuple-element.9.refs_1_, bf16[2304,384]{1,0:T(8,128)(2,1)S(1)} %get-tuple-element.10.refs_2_, ...), custom_call_target="tpu_custom_call" | custom-call | tf_op jit(solution)/shard_map/pallas_call | solution.py:436

commit v3 on v2

--- a/solution.py
+++ b/solution.py
@@ -63,42 +63,56 @@
     ((2, 1), (2, 2), (1, 2), (2, -1)),
     ((0, -1), (1, 1), (-1, 1), (-1, 2)),
 )
-RING = {1: 1, 2: 1, 3: 1, 4: 1, -1: -1, -2: -1, -3: -1}
-SHORT = {1: 1, 2: 2, 3: 1, 4: 2, -1: -1, -2: -1, -3: -2}
-SUM_TREE = (RING, RING, RING, RING)
-SPREAD_TREE = (RING, RING, RING, RING)
+SUM_TREE = (
+    {1: 1, 2: 1, 3: 1, 4: 1, -1: -1, -2: -1, -3: -1},
+    {1: 1, 2: 1, 3: 1, 4: 1, -1: -1, -2: -1, -3: -1},
+    {1: 1, 2: 1, 3: 1, 4: 1, -1: -1, -2: -1, -3: -1},
+    {1: 1, 2: 1, 3: 1, 4: 1, -1: -1, -2: -1, -3: -1},
+    {1: 1, 2: 1, 3: 1, 4: 1, -1: -1, -2: -1, -3: -1},
+    {1: 1, 2: 1, 3: 1, 4: 1, -1: -1, -2: -1, -3: -1},
+    {1: 1, 2: 1, 3: 1, 4: 1, -1: -1, -2: -1, -3: -1},
+    {1: 1, 2: 1, 3: 1, 4: 1, -1: -1, -2: -1, -3: -1},
+)
+SUM_SIGN = (1, 1, -1, -1, 1, 1, -1, -1)
+SPREAD_TREE = (
+    {1: 1, 2: 1, 3: 1, 4: 1, -1: -1, -2: -1, -3: -1},
+    {1: 1, 2: 1, 3: 1, 4: 1, -1: -1, -2: -1, -3: -1},
+    {1: 1, 2: 1, 3: 1, 4: 1, -1: -1, -2: -1, -3: -1},
+    {1: 1, 2: 1, 3: 1, 4: 1, -1: -1, -2: -1, -3: -1},
+)
+SPREAD_SIGN = (1, -1, 1, -1)
 ORDER = (
-    ("Y",), ("G", 1, 0), ("G", 3, 0), ("G", 2, 0), ("G", 12, 0),
-    ("G", 1, 1), ("G", 3, 1), ("G", 2, 1), ("G", 12, 1), ("F", 0, 0),
-    ("G", 7, 0), ("G", 4, 0), ("G", 6, 0), ("G", 5, 0), ("F", 0, 3),
-    ("R", 0, -3), ("R", 0, 4), ("X", 0), ("G", 14, 0), ("G", 7, 1),
-    ("G", 13, 0), ("G", 5, 1), ("G", 4, 1), ("G", 6, 1), ("R", 0, -2),
-    ("G", 15, 0), ("G", 11, 0), ("R", 0, 3), ("F", 1, 0), ("G", 13, 1),
-    ("G", 14, 1), ("F", 1, 3), ("G", 8, 0), ("G", 15, 1), ("R", 1, 4),
-    ("R", 1, -3), ("R", 0, -1), ("X", 1), ("G", 10, 0), ("G", 11, 1),
-    ("R", 0, 2), ("G", 9, 0), ("F", 3, 0), ("G", 10, 1), ("F", 3, 3),
-    ("G", 8, 1), ("R", 1, -2), ("R", 1, 3), ("R", 3, -3), ("R", 3, 4),
-    ("X", 3), ("R", 0, 1), ("G", 9, 1), ("F", 2, 0), ("R", 1, -1),
-    ("R", 1, 2), ("F", 2, 3), ("R", 2, 4), ("R", 3, -2), ("R", 2, -3),
-    ("A", 0), ("R", 3, 3), ("X", 2), ("R", 1, 1), ("R", 2, 3),
-    ("R", 2, -2), ("R", 3, -1), ("Z", 0, -1), ("Z", 0, 1), ("R", 3, 2),
-    ("R", 2, 2), ("A", 1), ("R", 2, -1), ("Z", 0, 2), ("Z", 0, -2),
-    ("R", 2, 1), ("R", 3, 1), ("Z", 1, -1), ("Z", 1, 1), ("Z", 0, 3),
-    ("A", 2), ("Z", 0, -3), ("Z", 1, -2), ("A", 3), ("Z", 0, 4),
-    ("C", 0), ("Z", 1, 2), ("S", 0), ("W", 0, 0), ("Z", 2, 1),
-    ("Z", 2, -1), ("W", 0, 1), ("W", 0, 2), ("Z", 1, -3), ("Z", 3, 1),
-    ("O", 0), ("Z", 3, -1), ("Z", 1, 3), ("T", 2), ("W", 0, 3),
-    ("W", 0, 4), ("Z", 2, 2), ("Z", 2, -2), ("W", 0, 5), ("Z", 3, 2),
-    ("Z", 3, -2), ("Z", 1, 4), ("C", 1), ("S", 1), ("Z", 2, 3),
-    ("Z", 2, -3), ("W", 1, 0), ("W", 1, 1), ("Z", 3, 3), ("W", 1, 2),
-    ("O", 1), ("Z", 3, -3), ("T", 4), ("T", 6), ("W", 1, 3),
-    ("Z", 2, 4), ("C", 2), ("S", 2), ("Z", 3, 4), ("C", 3),
-    ("S", 3), ("W", 1, 4), ("O", 2), ("T", 9), ("T", 10),
-    ("T", 8), ("T", 3), ("T", 11), ("T", 1), ("O", 3),
-    ("T", 12), ("T", 15), ("T", 13), ("W", 1, 5), ("W", 2, 0),
-    ("W", 2, 1), ("W", 2, 2), ("W", 2, 3), ("W", 2, 4), ("W", 2, 5),
-    ("W", 3, 0), ("W", 3, 1), ("W", 3, 2), ("T", 5), ("T", 14),
-    ("W", 3, 3), ("W", 3, 4), ("W", 3, 5), ("T", 7), ("E",),
+    ("Y",), ("I",), ("G", 1, 0), ("G", 3, 0), ("G", 2, 0), ("G", 12, 0),
+    ("F", 0, 0), ("R", 0, 4), ("R", 0, -3), ("G", 1, 1), ("G", 3, 1), ("G", 12, 1),
+    ("G", 2, 1), ("X", 0), ("F", 0, 3), ("R", 1, 4), ("R", 1, -3), ("G", 4, 0),
+    ("G", 6, 0), ("G", 7, 0), ("G", 5, 0), ("R", 0, 3), ("R", 0, -2), ("F", 1, 0),
+    ("X", 1), ("R", 1, -2), ("G", 5, 1), ("G", 13, 0), ("G", 7, 1), ("R", 1, 3),
+    ("R", 2, 4), ("R", 2, -3), ("G", 14, 0), ("R", 0, 2), ("R", 0, -1), ("G", 4, 1),
+    ("G", 6, 1), ("G", 11, 0), ("G", 15, 0), ("F", 1, 3), ("R", 1, -1), ("R", 1, 2),
+    ("R", 3, 4), ("R", 3, -3), ("F", 3, 0), ("G", 13, 1), ("G", 14, 1), ("R", 6, 4),
+    ("R", 2, -2), ("R", 6, -3), ("R", 2, 3), ("R", 0, 1), ("X", 3), ("G", 11, 1),
+    ("G", 15, 1), ("G", 10, 0), ("F", 3, 3), ("R", 1, 1), ("R", 7, 4), ("R", 3, 3),
+    ("R", 7, -3), ("R", 3, -2), ("G", 8, 0), ("G", 9, 0), ("R", 6, 3), ("R", 2, -1),
+    ("G", 10, 1), ("R", 2, 2), ("R", 6, -2), ("F", 2, 0), ("R", 4, -3), ("R", 4, 4),
+    ("X", 2), ("G", 8, 1), ("A", 0), ("R", 7, 3), ("G", 9, 1), ("R", 7, -2),
+    ("R", 3, 2), ("R", 3, -1), ("R", 6, 2), ("F", 2, 3), ("R", 5, 4), ("R", 5, -3),
+    ("R", 2, 1), ("R", 6, -1), ("R", 4, -2), ("R", 4, 3), ("Z", 0, 1), ("Z", 0, -1),
+    ("R", 7, 2), ("R", 7, -1), ("R", 3, 1), ("R", 5, 3), ("R", 6, 1), ("R", 5, -2),
+    ("R", 4, 2), ("R", 4, -1), ("Z", 0, -2), ("Z", 0, 2), ("R", 5, 2), ("R", 7, 1),
+    ("A", 1), ("R", 4, 1), ("R", 5, -1), ("Z", 0, -3), ("R", 5, 1), ("Z", 0, 3),
+    ("A", 3), ("Z", 1, 1), ("Z", 1, -1), ("A", 2), ("Z", 0, 4), ("C", 0),
+    ("S", 0), ("Z", 3, 1), ("Z", 3, -1), ("Z", 1, 2), ("O", 0), ("Z", 1, -2),
+    ("T", 2), ("Z", 2, -1), ("Z", 2, 1), ("Z", 3, 2), ("Z", 3, -2), ("Z", 1, 3),
+    ("Z", 1, -3), ("Z", 2, -2), ("Z", 2, 2), ("Z", 3, 3), ("Z", 3, -3), ("Z", 1, 4),
+    ("C", 1), ("S", 1), ("W", 1, 4), ("W", 1, 3), ("W", 1, 5), ("W", 0, 5),
+    ("Z", 2, 3), ("Z", 2, -3), ("O", 1), ("T", 6), ("T", 4), ("Z", 3, 4),
+    ("C", 3), ("S", 3), ("W", 0, 4), ("W", 1, 0), ("W", 0, 0), ("W", 1, 1),
+    ("O", 3), ("T", 12), ("T", 15), ("T", 13), ("Z", 2, 4), ("C", 2),
+    ("S", 2), ("W", 2, 4), ("W", 3, 4), ("W", 2, 0), ("W", 3, 0), ("O", 2),
+    ("T", 10), ("T", 3), ("T", 9), ("T", 8), ("T", 11), ("W", 2, 5),
+    ("W", 3, 5), ("T", 1), ("W", 0, 3), ("W", 2, 3), ("W", 3, 3), ("W", 1, 2),
+    ("W", 0, 2), ("W", 2, 2), ("W", 3, 2), ("W", 0, 1), ("W", 2, 1), ("W", 3, 1),
+    ("T", 7), ("T", 14), ("T", 5), ("E",),
 )
 SLOT = {p: i for i, p in enumerate(p for chunk in CHUNK_PIECES for p in chunk)}
 OWN = SLOT[0, 0]
@@ -113,7 +127,7 @@
 PARENT = {p: less(p, d) for p, d in REDUCE.items()}
 CHILDREN = {p: [q for q in REDUCE if PARENT[q] == p] for p in SLOT}
 PIECES = {s: p for p, s in SLOT.items()}
-OFFSETS = tuple(RING)
+OFFSETS = (1, 2, 3, 4, -1, -2, -3)
 NT = (((1,), (1,)), ((), ()))
 W_ORDER = [step[1] for step in ORDER if step[0] == "W" and step[2] == 0]
 
@@ -125,7 +139,7 @@
 def kernel(
     x_hbm, wg_hbm, wu_hbm, wd_hbm, c_hbm,
     gi_out, gg_out, gu_out, gd_out,
-    own, stage, xc, xt, wcat, wt, wd, part, rs_s, rs_r, agb, act, ht,
+    own, stage, xc, xt, wcat, wt, wd, part, gu_s, gu_r, dh_s, dh_r, agb, act, ht,
     gi_own, gi_s, gi_r, tr_s, tr_r, fin, acc_gu, acc_d,
     load_sem, stage_sem, ag_ss, ag_rs, sib_ss, sib_rs, rs_ss, rs_rs, za_ss, za_rs,
     gx_ss, gx_rs, tr_ss, tr_rs, fin_sem,
@@ -176,42 +190,48 @@
         pl.semaphore_signal(barrier, inc=1, device_id=dev, device_id_type=MESH)
     pl.semaphore_wait(barrier, len(greet))
 
-    loads[0].wait()
-    loads[1].wait()
-    swap = send(own.at[1 - c], stage, stage_sem.at[0], stage_sem.at[1], sibling)
-    start(swap)
-    swap.wait_recv()
-    mine, other = own[c].astype(F32), stage[...].astype(F32)
-    first = c == 0
-    xc[c, OWN] = jnp.concatenate(
-        [jnp.where(first, mine, other), jnp.where(first, other, mine)], axis=0
-    ).astype(BF16)
-
-    def share(a, s, half):
-        part_of = xc.at[a, s, :, pl.ds(half * HALF, HALF)]
-        return send(part_of, part_of, sib_ss.at[s, half], sib_rs.at[s, half], sibling)
-
-    def hop(p, half):
-        s, d, cols = SLOT[p], COMES[p], pl.ds(half * HALF, HALF)
+    ours = pl.ds(pl.multiple_of(c * HALF, 128), HALF)
+    theirs = pl.ds(pl.multiple_of((1 - c) * HALF, 128), HALF)
+
+    def swap(a):
+        return send(own.at[a, :, theirs], stage.at[a], stage_sem.at[0, a], stage_sem.at[1, a], sibling)
+
+    for a in (0, 1):
+        loads[a].wait()
+        start(swap(a))
+
+    def share(a, s, cols):
+        block = xc.at[a, s, :, cols]
+        return send(block, block, sib_ss.at[s, a], sib_rs.at[s, a], sibling)
+
+    def hop(p, a):
+        s, d = SLOT[p], COMES[p]
         return send(
-            xc.at[c, SLOT[SOURCE[p]], :, cols], xc.at[c, s, :, cols],
-            ag_ss.at[s, half], ag_rs.at[s, half], at((-d[0], -d[1])),
+            xc.at[a, SLOT[SOURCE[p]], :, ours], xc.at[a, s, :, ours],
+            ag_ss.at[s, a], ag_rs.at[s, a], at((-d[0], -d[1])),
         )
 
-    def forward(q, half):
+    def forward(q, a):
         for p, _ in GATHER:
             if SOURCE[p] == q:
-                start(hop(p, half))
-
-    def gather(s, half):
-        hop(PIECES[s], half).wait_recv()
-        forward(PIECES[s], half)
-        start(share(c, s, half))
-
-    for half in (0, 1):
-        forward((0, 0), half)
-    for half in (0, 1):
-        start(share(c, OWN, half))
+                start(hop(p, a))
+
+    def gather(s, a):
+        hop(PIECES[s], a).wait_recv()
+        forward(PIECES[s], a)
+        start(share(a, s, ours))
+
+    def begin(a):
+        swap(a).wait_recv()
+        mine, other = own[a, :, ours].astype(F32), stage[a].astype(F32)
+        first = c == 0
+        xc[a, OWN, :, ours] = jnp.concatenate(
+            [jnp.where(first, mine, other), jnp.where(first, other, mine)], axis=0
+        ).astype(BF16)
+        forward((0, 0), a)
+        start(share(a, OWN, ours))
+
+    begin(0)
 
     def flip_weights():
         for copy in loads[2:]:
@@ -236,43 +256,43 @@
         return xc[a, pl.ds(PER * k, PER)].reshape(ROWS, DM)
 
     def product(k, n):
+        a = 0 if n == 0 else 1
+        for i in range(PER * k, PER * k + PER):
+            share(a, i, theirs).wait_recv()
         if n == 0:
-            for i in range(PER * k, PER * k + PER):
-                for half in (0, 1):
-                    share(1 - c, i, half).wait_recv()
             part[k, :, :, pl.ds(0, 2 * FD)] = dot(rows_of(0, k), wcat[...]).reshape(NZ, BLK, 2 * FD)
         else:
             part[k, :, :, pl.ds(2 * FD, FD)] = dot(rows_of(1, k), wd[...], NT).reshape(NZ, BLK, FD)
 
-    def sign(k):
-        return 1 if k % 2 == 0 else -1
-
-    def sum_copy(k, o):
-        m = OFFSETS.index(o)
-        dev = {"mp": zat(sign(k) * SUM_TREE[k][o])}
-        return send(rs_s.at[k, m], rs_r.at[k, m], rs_ss.at[k, m], rs_rs.at[k, m], dev)
-
-    def sum_at(k, o):
-        value = part[k, zat(sign(k) * o)]
-        for q, d in SUM_TREE[k].items():
+    def sum_copy(u, o):
+        k, j, m = u // 2, u % 2, OFFSETS.index(o)
+        src, dst = (dh_s, dh_r) if j else (gu_s, gu_r)
+        dev = {"mp": zat(SUM_SIGN[u] * SUM_TREE[u][o])}
+        return send(src.at[k, m], dst.at[k, m], rs_ss.at[u, m], rs_rs.at[u, m], dev)
+
+    def sum_at(u, o):
+        k, j = u // 2, u % 2
+        cols, landed = (pl.ds(2 * FD, FD), dh_r) if j else (pl.ds(0, 2 * FD), gu_r)
+        value = part[k, zat(SUM_SIGN[u] * o), :, cols]
+        for q, d in SUM_TREE[u].items():
             if q - d == o:
-                sum_copy(k, q).wait_recv()
-                value = value + rs_r[k, OFFSETS.index(q)].astype(F32)
+                sum_copy(u, q).wait_recv()
+                value = value + landed[k, OFFSETS.index(q)].astype(F32)
         return value
 
-    def reduce(k, o):
-        rs_s[k, OFFSETS.index(o)] = sum_at(k, o).astype(BF16)
-        start(sum_copy(k, o))
+    def reduce(u, o):
+        (dh_s if u % 2 else gu_s)[u // 2, OFFSETS.index(o)] = sum_at(u, o).astype(BF16)
+        start(sum_copy(u, o))
 
     def spread_copy(k, o):
         m, d = OFFSETS.index(o), SPREAD_TREE[k][o]
-        block = agb.at[k, zat(-sign(k) * (o - d))]
-        return send(block, block, za_ss.at[k, m], za_rs.at[k, m], {"mp": zat(sign(k) * d)})
+        block = agb.at[k, zat(SPREAD_SIGN[k] * (o - d))]
+        return send(block, block, za_ss.at[k, m], za_rs.at[k, m], {"mp": zat(-SPREAD_SIGN[k] * d)})
 
     def spread_wait(k, o):
         m, d = OFFSETS.index(o), SPREAD_TREE[k][o]
-        block = agb.at[k, zat(-sign(k) * o)]
-        send(block, block, za_ss.at[k, m], za_rs.at[k, m], {"mp": zat(sign(k) * d)}).wait_recv()
+        block = agb.at[k, zat(SPREAD_SIGN[k] * o)]
+        send(block, block, za_ss.at[k, m], za_rs.at[k, m], {"mp": zat(-SPREAD_SIGN[k] * d)}).wait_recv()
 
     def spread_on(k, q):
         for o, d in SPREAD_TREE[k].items():
@@ -284,8 +304,8 @@
         spread_on(k, o)
 
     def activate(k):
-        total = sum_at(k, 0)
-        gate, up, dhid = total[:, :FD], total[:, FD : 2 * FD], total[:, 2 * FD :]
+        both, dhid = sum_at(2 * k, 0), sum_at(2 * k + 1, 0)
+        gate, up = both[:, :FD], both[:, FD:]
         sig = jax.nn.sigmoid(gate)
         agb[k, z] = jnp.concatenate(
             [
@@ -359,18 +379,19 @@
 
     def finish():
         gi_own[OWN] = tree_sum((0, 0))
-        theirs = pl.ds(pl.multiple_of((1 - c) * SHARD, 8), SHARD)
-        ours = pl.ds(pl.multiple_of(c * SHARD, 8), SHARD)
-        fin[1] = gi_own[OWN, theirs, :].astype(BF16)
+        sent_rows = pl.ds(pl.multiple_of((1 - c) * SHARD, 8), SHARD)
+        kept_rows = pl.ds(pl.multiple_of(c * SHARD, 8), SHARD)
+        fin[1] = gi_own[OWN, sent_rows, :].astype(BF16)
         copy = send(fin.at[1], fin.at[0], fin_sem.at[0], fin_sem.at[1], sibling)
         start(copy)
-        gi_out[:, pl.ds(pl.multiple_of(c * HALF, 128), HALF)] = gi_own[OWN, ours, :].astype(BF16)
+        gi_out[:, ours] = gi_own[OWN, kept_rows, :].astype(BF16)
         copy.wait_recv()
-        gi_out[:, pl.ds(pl.multiple_of((1 - c) * HALF, 128), HALF)] = fin[0]
+        gi_out[:, theirs] = fin[0]
 
     steps = {
         "G": gather, "F": product, "R": reduce, "A": activate, "Z": spread, "C": collect,
         "S": their_half, "O": our_half, "T": tree, "W": weight_grads, "E": finish, "X": flip_inputs, "Y": flip_weights,
+        "I": lambda: begin(1),
     }
     for step, *numbers in ORDER:
         steps[step](*numbers)
@@ -399,15 +420,17 @@
         out_specs=(pl.BlockSpec(memory_space=pltpu.VMEM),) * 4,
         scratch_shapes=[
             pltpu.VMEM((2, SHARD, DM), BF16),
-            pltpu.VMEM((SHARD, DM), BF16),
+            pltpu.VMEM((2, SHARD, HALF), BF16),
             pltpu.VMEM((2, slots, PIECE, DM), BF16),
             pltpu.VMEM((CHUNKS, DM, 256), BF16),
             pltpu.VMEM((DM, 2 * FD), BF16),
             pltpu.VMEM((2 * FD, DM), BF16),
             pltpu.VMEM((FD, DM), BF16),
             pltpu.VMEM((CHUNKS, NZ, BLK, 3 * FD), F32),
-            pltpu.VMEM((CHUNKS, offsets, BLK, 3 * FD), BF16),
-            pltpu.VMEM((CHUNKS, offsets, BLK, 3 * FD), BF16),
+            pltpu.VMEM((CHUNKS, offsets, BLK, 2 * FD), BF16),
+            pltpu.VMEM((CHUNKS, offsets, BLK, 2 * FD), BF16),
+            pltpu.VMEM((CHUNKS, offsets, BLK, FD), BF16),
+            pltpu.VMEM((CHUNKS, offsets, BLK, FD), BF16),
             pltpu.VMEM((CHUNKS, NZ, BLK, 3 * FD), BF16),
             pltpu.VMEM((CHUNKS, ROWS, 3 * FD), BF16),
             pltpu.VMEM((CHUNKS, FD, 256), BF16),
@@ -420,10 +443,10 @@
             pltpu.VMEM((DM, 2 * FD), F32),
             pltpu.VMEM((FD, DM), F32),
             dma((5,)),
-            dma((2,)),
+            dma((2, 2)),
             dma((slots, 2)), dma((slots, 2)),
             dma((slots, 2)), dma((slots, 2)),
-            dma((CHUNKS, offsets)), dma((CHUNKS, offsets)),
+            dma((2 * CHUNKS, offsets)), dma((2 * CHUNKS, offsets)),
             dma((CHUNKS, offsets)), dma((CHUNKS, offsets)),
             dma((CHUNKS,)), dma((CHUNKS,)),
             dma((slots,)), dma((slots,)),

time: 92 us -> 91 us (0.989)
  Pallas kernels: 91.1 us -> 90.1 us
    pallas_call x1, Pallas kernels: 88.7 us -> 87.6 us  [shards(): pl.pallas_call(kernel, out_shape=tuple((pltpu.VMEM(shape, BF16) for shape...]
where the time goes in v3:
time: 91 us; the launch traced here: 90.9 us
  Pallas kernels  90.1 us (99%)
    pallas_call x1, Pallas kernels, shards(): pl.pallas_call(kernel, out_shape=tuple((pltpu.VMEM(shape, BF16) for shape...  87.6 us
    pallas_call x1, Pallas kernels, shards(): pl.pallas_call(store, out_shape=tuple((jax.ShapeDtypeStruct(shape, BF16)...  2.45 us

profile of v3, /device:TPU:1, one launch (start us, length us, event | category | flops | bytes accessed | tf_op | source)
XLA Modules:
  0.0 90.9 jit_solution(5974006725330142211)
XLA Ops:
  0.6 87.6 %shard_map.84 = (bf16[24,2304]{1,0:T(8,128)(2,1)S(1)}, bf16[2304,384]{1,0:T(8,128)(2,1)S(1)}, bf16[2304,384]{1,0:T(8,128)(2,1)S(1)}, bf16[384,2304]{1,0:T(8,128)(2,1)S(1)}) custom-call(bf16[24,2304]{1,0:T(8,128)(2,1)} %x_hbm.1, bf16[2304,384]{1,0:T(8,128)(2,1)} %wg_hbm.1, bf16[2304,384]{1,0:T(8,128)(2,1)} %wu_hbm.1, bf16[384,2304]{1,0:T(8,128)(2,1)} %wd_hbm.1, ...), custom_call_target="tpu_custom_call" | custom-call | tf_op jit(solution)/shard_map/pallas_call | solution.py:416
  88.3 2.4 %shard_map.85 = (bf16[24,2304]{1,0:T(8,128)(2,1)}, bf16[2304,384]{1,0:T(8,128)(2,1)}, bf16[2304,384]{1,0:T(8,128)(2,1)}, bf16[384,2304]{1,0:T(8,128)(2,1)}) custom-call(bf16[24,2304]{1,0:T(8,128)(2,1)S(1)} %get-tuple-element.8.refs_0_, bf16[2304,384]{1,0:T(8,128)(2,1)S(1)} %get-tuple-element.9.refs_1_, bf16[2304,384]{1,0:T(8,128)(2,1)S(1)} %get-tuple-element.10.refs_2_, ...), custom_call_target="tpu_custom_call" | custom-call | tf_op jit(solution)/shard_map/pallas_call | solution.py:459

commit v4 on v3

--- a/solution.py
+++ b/solution.py
@@ -378,6 +378,9 @@
                 acc_d[:, cols] = value
 
     def finish():
+        for copy in sent:
+            copy.wait_send()
+        sent.clear()
         gi_own[OWN] = tree_sum((0, 0))
         sent_rows = pl.ds(pl.multiple_of((1 - c) * SHARD, 8), SHARD)
         kept_rows = pl.ds(pl.multiple_of(c * SHARD, 8), SHARD)

time: 91 us -> 90.7 us (level)
  no operation moved by 1% of the time
where the time goes in v4:
time: 90.7 us; the launch traced here: 90.6 us
  Pallas kernels  89.8 us (99%)
    pallas_call x1, Pallas kernels, shards(): pl.pallas_call(kernel, out_shape=tuple((pltpu.VMEM(shape, BF16) for shape...  87.4 us
    pallas_call x1, Pallas kernels, shards(): pl.pallas_call(store, out_shape=tuple((jax.ShapeDtypeStruct(shape, BF16)...  2.45 us

profile of v4, /device:TPU:1, one launch (start us, length us, event | category | flops | bytes accessed | tf_op | source)
XLA Modules:
  0.0 90.6 jit_solution(2376044782692992320)
XLA Ops:
  0.6 87.4 %shard_map.84 = (bf16[24,2304]{1,0:T(8,128)(2,1)S(1)}, bf16[2304,384]{1,0:T(8,128)(2,1)S(1)}, bf16[2304,384]{1,0:T(8,128)(2,1)S(1)}, bf16[384,2304]{1,0:T(8,128)(2,1)S(1)}) custom-call(bf16[24,2304]{1,0:T(8,128)(2,1)} %x_hbm.1, bf16[2304,384]{1,0:T(8,128)(2,1)} %wg_hbm.1, bf16[2304,384]{1,0:T(8,128)(2,1)} %wu_hbm.1, bf16[384,2304]{1,0:T(8,128)(2,1)} %wd_hbm.1, ...), custom_call_target="tpu_custom_call" | custom-call | tf_op jit(solution)/shard_map/pallas_call | solution.py:419
  88.0 2.4 %shard_map.85 = (bf16[24,2304]{1,0:T(8,128)(2,1)}, bf16[2304,384]{1,0:T(8,128)(2,1)}, bf16[2304,384]{1,0:T(8,128)(2,1)}, bf16[384,2304]{1,0:T(8,128)(2,1)}) custom-call(bf16[24,2304]{1,0:T(8,128)(2,1)S(1)} %get-tuple-element.8.refs_0_, bf16[2304,384]{1,0:T(8,128)(2,1)S(1)} %get-tuple-element.9.refs_1_, bf16[2304,384]{1,0:T(8,128)(2,1)S(1)} %get-tuple-element.10.refs_2_, ...), custom_call_target="tpu_custom_call" | custom-call | tf_op jit(solution)/shard_map/pallas_call | solution.py:462
